TPU v7x, 768 devices: a whole 4x8x12 slice. The times are simulated.
768 devices in a mesh: section: 4 (over y_lo), fsdp: 192 (over x, y_hi, z, core).
Axes of the slice: x: 4, y: 8 (y_hi: 2, y_lo: 4; y = y_hi * 4 + y_lo), z: 12, core: 2. Of those that a mesh axis runs over, the one named last changes fastest.
Arguments:
- hidden: bfloat16 [4, 24576, 4608], P('section', 'fsdp'), may hold values from -24 to 24
- gain: bfloat16 [4, 4608], P('section'), may hold values from 0.099609375 to 1.8984375
- key_grad: bfloat16 [4, 24576, 512], P('section', 'fsdp'), may hold values from -6 to 6
- residual_grad: bfloat16 [4, 24576, 4608], P('section', 'fsdp'), may hold values from -6 to 6
- key_weight: bfloat16 [4, 4608, 512], P('section', 'fsdp'), may hold values from -0.09375 to 0.09375
Outputs:
- passed_grad: bfloat16 [4, 24576, 4608], P('section', 'fsdp')
- weight_grad: float32 [4, 4608, 512], P('section', 'fsdp')
All inputs are finite; a program needn't handle non-finite values.
Results may differ from a plain program's by a relative error of at most 0.0029.
Values may be sent and summed in bfloat16 or wider, within the bound.
A program may use at most 64 MiB of HBM per device.

v0:
```python
import math

import jax
import jax.numpy as jnp
from jax import lax
from jax.sharding import PartitionSpec as P


def passed_along(x, axis, by):
    length = lax.axis_size(axis)
    pairs = [(i, i + by) for i in range(length) if 0 <= i + by < length]
    return lax.ppermute(x, axis, pairs)


def body(hidden, gain, key_grad, residual_grad, key_weight):
    x = hidden[0].astype(jnp.float32)
    g = gain[0].astype(jnp.float32)
    grads = key_grad[0]
    total_tokens = hidden.shape[1] * lax.axis_size("fsdp")
    scale = 1.0 / jnp.sqrt(jnp.mean(x * x, axis=-1, keepdims=True) + 1e-05)
    normed = (x * scale * g).astype(jnp.bfloat16)
    normed_grad = lax.dot_general(
        grads,
        lax.all_gather(key_weight[0], "fsdp", axis=0, tiled=True),
        (((1,), (1,)), ((), ())),
        preferred_element_type=jnp.float32,
    )
    weighted = normed_grad * g
    inner = jnp.mean(weighted * x, axis=-1, keepdims=True)
    result = (
        weighted * scale - x * inner * scale * scale * scale + residual_grad[0].astype(jnp.float32)
    )
    passed = passed_along(result.astype(jnp.bfloat16), "section", -1)
    summed = lax.psum_scatter(
        lax.dot_general(
            normed, grads, (((0,), (0,)), ((), ())), preferred_element_type=jnp.float32
        ),
        "fsdp",
        scatter_dimension=0,
        tiled=True,
    )
    grad_w = summed / math.sqrt(total_tokens)
    return (passed[None], grad_w[None])


def solution(mesh):
    return jax.shard_map(
        body,
        mesh=mesh,
        in_specs=(
            P("section", "fsdp", None),
            P("section", None),
            P("section", "fsdp", None),
            P("section", "fsdp", None),
            P("section", "fsdp", None),
        ),
        out_specs=(P("section", "fsdp", None), P("section", "fsdp", None)),
        check_vma=False,
    )
```

profile of v0, /device:TPU:1, one launch (start us, length us, event | category | flops | bytes accessed | tf_op | source)
XLA Modules:
  0.0 691.1 jit_solution(3788726950467967928)
XLA Ops:
  7.2 0.0 copy-start
  7.2 0.0 all-gather.3.cloned.1.call-start
  7.2 0.7 all-gather.3.cloned.1.call-update
  7.9 0.0 reduce-scatter.2.cloned.1.call-start
  8.0 0.8 convert_reduce_fusion
  8.7 0.0 copy-start.1
  8.8 201.7 %all-gather.3.cloned.1.call-done = bf16[1,4608,512]{2,1,0:T(8,128)(2,1)} async-done(((bf16[1,24,512]{2,1,0:T(8,128)(2,1)}), bf16[1,4608,512]{2,1,0:T(8,128)(2,1)}) %all-gather.3.cloned.1.call-update) | async-done | bytes 4718608 | tf_op jit(solution)/shard_map/all_gather | solution.py:24
  210.5 0.0 copy-done
  210.5 5.8 fusion.4
  216.3 0.0 copy-done.1
  216.3 5.1 fusion.15
  221.4 0.0 copy-start.2
  221.4 0.0 reduce-scatter.2.cloned.1.call-update
  221.4 1.2 copy-done.2
  222.7 2.5 fusion.11
  225.1 1.3 collective-permute-start
  226.4 27.9 %collective-permute-done = bf16[128,4608]{1,0:T(8,128)(2,1)S(1)} collective-permute-done((bf16[128,4608]{1,0:T(8,128)(2,1)S(1)}, bf16[128,4608]{1,0:T(8,128)(2,1)S(1)}, u32[]{:S(2)}, u32[]{:S(2)}) %collective-permute-start) | collective-permute-done | bytes 1179680 | tf_op jit(solution)/shard_map/ppermute | solution.py:12
  254.4 427.5 %reduce-scatter.2.cloned.1.call-done = f32[24,512]{1,0:T(8,128)} async-done(((f32[4608,512]{1,0:T(8,128)}), f32[24,512]{1,0:T(8,128)}) %reduce-scatter.2.cloned.1.call-update) | async-done | bytes 49168 | tf_op jit(solution)/shard_map/reduce_scatter | solution.py:34
  681.8 1.4 multiply_bitcast_fusion
  683.3 1.0 copy.8
  (2 shorter events, 0.0 us)
Async XLA Ops:
  7.2 203.3 %copy-start = (bf16[1,128,512]{2,1,0:T(8,128)(2,1)S(1)}, bf16[1,128,512]{2,1,0:T(8,128)(2,1)}, u32[]{:S(2)}) copy-start(bf16[1,128,512]{2,1,0:T(8,128)(2,1)} %param.7) | copy-start | bytes 393220
  7.2 203.3 %all-gather.3.cloned.1.call-start = ((), (), s32[]{:S(2)}) async-start(), calls=%async_computation.2 | async-start | bytes 4743168 | tf_op jit(solution)/shard_map/all_gather | solution.py:24
  7.9 673.9 %reduce-scatter.2.cloned.1.call-start = ((), (), s32[]{:S(2)}) async-start(), calls=%async_computation.1 | async-start | bytes 9486336 | tf_op jit(solution)/shard_map/reduce_scatter | solution.py:34
  8.7 207.5 %copy-start.1 = (bf16[1,128,4608]{2,1,0:T(8,128)(2,1)S(1)}, bf16[1,128,4608]{2,1,0:T(8,128)(2,1)}, u32[]{:S(2)}) copy-start(bf16[1,128,4608]{2,1,0:T(8,128)(2,1)} %param.5) | copy-start | bytes 3538948
  221.4 1.3 copy-start.2
  225.1 29.2 %collective-permute-start = (bf16[128,4608]{1,0:T(8,128)(2,1)S(1)}, bf16[128,4608]{1,0:T(8,128)(2,1)S(1)}, u32[]{:S(2)}, u32[]{:S(2)}) collective-permute-start(bf16[128,4608]{1,0:T(8,128)(2,1)S(1)} %fusion.11), channel_id=1, source_target_pairs={{192,0},{384,192},{576,384},{193,1},{385,193},{577,385},{194,2},{3... | collective-permute-start | bytes 3538952 | tf_op jit(solution)/shard_map/ppermute | solution.py:12
Sparse Core Ops, SparseCore 0:
  13.6 196.8 all-gather.2
  221.6 460.2 reduce-scatter.1
where the time goes:
time: 698 us; the launch traced here: 691 us
  waiting for transfers between devices  658 us (94%)
  between operations  14.1 us (2%)
  matrix products  10.9 us (2%)
    reduce_scatter x1, waiting for transfers between devices, body(): lax.psum_scatter(lax.dot_general(normed, grads, (((0,), (0,)), ((), ())),...  427 us
    all_gather x1, waiting for transfers between devices, body(): lax.all_gather(key_weight[0], 'fsdp', axis=0, tiled=True)  202 us
    ppermute x1, waiting for transfers between devices, passed_along(): return lax.ppermute(x, axis, pairs)  27.9 us
  transfers between devices with their start and end apart: 3, of which 3 were waited for; matrix products, arithmetic and copies ran while one was open for 0% of the time, Pallas kernels for 0%

commit v1 on v0

v1 whole, which is shorter than its diff:
```python
import functools
import math

import jax
import jax.numpy as jnp
from jax import lax
from jax.experimental import pallas as pl
from jax.experimental.pallas import tpu as pltpu
from jax.sharding import PartitionSpec as P

MESH = pl.DeviceIdType.MESH
NX, NY, NZ, NS = 4, 2, 12, 4
RIGHT, LEFT = NZ // 2, (NZ - 1) // 2
TOK, KW, ROWS = 128, 512, 24
HALF = KW // 2
COLS = NY * NZ * 2 * ROWS
D = NX * COLS
TILE = 384
TILES = COLS // TILE
PAIRS = TILE // (2 * ROWS)
CHUNK = 16
CHUNKS = TOK // CHUNK
LAG = 1


def kernel(
    total_tokens,
    hidden,
    gain,
    key_grad,
    residual,
    key_weight,
    passed,
    grad_w,
    hid,
    res,
    grads,
    gains,
    scales,
    zeros,
    pair,
    weight,
    normed_out,
    normed_in,
    grads_in,
    part,
    part_in,
    land,
    across,
    normed_grad,
    result,
    load_sem,
    pair_sem,
    y_sem,
    x_send,
    x_recv,
    z_send,
    z_recv,
    share_send,
    share_recv,
    grads_send,
    grads_recv,
    normed_send,
    normed_recv,
    part_send,
    part_recv,
    sum_send,
    sum_recv,
    across_sem,
    pass_send,
    pass_recv,
):
    s = lax.axis_index("section")
    f = lax.axis_index("fsdp")
    core = lax.rem(f, 2)
    z = lax.rem(f // 2, NZ)
    y = lax.rem(f // (2 * NZ), NY)
    x = f // (2 * NZ * NY)

    def at(x_, y_, z_, core_):
        return (s, ((x_ * NY + y_) * NZ + z_) * 2 + core_)

    def shift_z(by):
        return lax.rem(z + (by + 2 * NZ), NZ)

    sibling = at(x, y, z, 1 - core)
    mirror = at(x, 1 - y, z, core)
    right = at(x, y, shift_z(1), core)
    left = at(x, y, shift_z(-1), core)
    others = [at(lax.rem(x + k, NX), y, z, core) for k in range(1, NX)]
    before, after = (s - 1, f), (s + 1, f)

    def remote(src, dst, send, recv, device):
        copy = pltpu.make_async_remote_copy(
            src_ref=src,
            dst_ref=dst,
            send_sem=send,
            recv_sem=recv,
            device_id=device,
            device_id_type=MESH,
        )
        return copy

    load_hidden = pltpu.make_async_copy(hidden.at[0], hid, load_sem.at[0])
    load_grads = pltpu.make_async_copy(key_grad.at[0], grads, load_sem.at[1])
    load_residual = pltpu.make_async_copy(residual.at[0], res, load_sem.at[2])
    load_hidden.start()
    load_grads.start()
    load_residual.start()

    barrier = pltpu.get_barrier_semaphore()
    for device in [sibling, mirror, right, left] + others:
        pl.semaphore_signal(barrier, 1, device_id=device, device_id_type=MESH)

    @pl.when(s < NS - 1)
    def _():
        pl.semaphore_signal(barrier, 1, device_id=after, device_id_type=MESH)

    pair[core] = key_weight[0].astype(jnp.float32)
    gains[...] = gain[...].astype(jnp.float32)
    pl.semaphore_wait(barrier, 4 + len(others) + jnp.minimum(s, 1))

    sent = []

    def start(copy):
        copy.start()
        sent.append(copy)
        return copy

    swap = start(remote(pair.at[core], pair.at[core], pair_sem.at[0], pair_sem.at[1], sibling))
    swap.wait_recv()
    block = pair[...].reshape(2 * ROWS, KW)
    weight[core, x, y, z] = jnp.where(core == 0, block[:, :HALF], block[:, HALF:]).astype(jnp.bfloat16)

    def own(plane):
        return weight.at[core, x, plane, z]

    def spread_x(plane, index):
        return [
            start(remote(own(plane), own(plane), x_send.at[index, k], x_recv.at[index, k], others[k]))
            for k in range(NX - 1)
        ]

    planes = [y, 1 - y]
    to_mirror = start(remote(own(y), own(y), y_sem.at[0], y_sem.at[1], mirror))
    x_copies = [spread_x(y, 0), None]

    load_grads.wait()
    grads_copies = [
        start(remote(grads, grads_in.at[x], grads_send.at[k], grads_recv.at[k], others[k]))
        for k in range(NX - 1)
    ]
    grads_in[x] = grads[...]

    load_hidden.wait()

    @pl.loop(0, CHUNKS)
    def _(c):
        rows = pl.ds(pl.multiple_of(c * CHUNK, CHUNK), CHUNK)
        total = jnp.zeros((CHUNK, 1), jnp.float32)
        for j in range(NX):
            h = hid[rows, pl.ds(j * COLS, COLS)].astype(jnp.float32)
            total += jnp.sum(h * h, axis=-1, keepdims=True)
        scale = 1.0 / jnp.sqrt(total / D + 1e-05)
        scales[rows, :] = jnp.broadcast_to(scale, (CHUNK, 128))
        for j in range(NX):
            h = hid[rows, pl.ds(j * COLS, COLS)].astype(jnp.float32)
            normed = h * scale * gains[:, pl.ds(j * COLS, COLS)]
            normed_out[j, rows, :] = normed.astype(jnp.bfloat16)

    def spread_normed():
        copies = []
        for k in range(NX - 1):
            to = lax.rem(x + k + 1, NX)
            copies.append(
                start(
                    remote(normed_out.at[to], normed_in.at[x], normed_send.at[k], normed_recv.at[k], others[k])
                )
            )
        normed_in[x] = normed_out[x]
        return copies

    def slot(index, by):
        return weight.at[core, :, planes[index], shift_z(by)]

    def share(index, by, order):
        return start(
            remote(slot(index, by), slot(index, by), share_send.at[index, order], share_recv.at[index, order], sibling)
        )

    shares, ring = [], {}

    def ring_step(index, step):
        if step == 0:
            if index == 1:
                to_mirror.wait_recv()
                x_copies[1] = spread_x(planes[1], 1)
            for copy in x_copies[index]:
                copy.wait_recv()
        for way, (device, steps, sign) in enumerate(((right, RIGHT, -1), (left, LEFT, 1))):
            if 0 < step <= steps:
                ring[way, index, step - 1].wait_recv()
            if step < steps:
                ring[way, index, step] = start(
                    remote(
                        slot(index, sign * step),
                        slot(index, sign * step),
                        z_send.at[way, index, step],
                        z_recv.at[way, index, step],
                        device,
                    )
                )
            if step == 0 and way == 0:
                shares.append(share(index, 0, 0))
            if 0 < step <= steps:
                shares.append(share(index, sign * step, step if way == 0 else RIGHT + step))

    def part_tile(t):
        lhs = normed_in[:, :, pl.ds(t * TILE, TILE)].reshape(NX * TOK, TILE)
        product = lax.dot_general(
            lhs,
            grads_in[...].reshape(NX * TOK, KW),
            (((0,), (0,)), ((), ())),
            preferred_element_type=jnp.float32,
        )
        part[pl.ds(t * PAIRS, PAIRS)] = product.reshape(PAIRS, 2, ROWS, KW)
        return start(
            remote(
                part.at[pl.ds(t * PAIRS, PAIRS), 1 - core],
                part_in.at[pl.ds(t * PAIRS, PAIRS)],
                part_send.at[t],
                part_recv.at[t],
                sibling,
            )
        )

    part_copies = []
    for turn in range(RIGHT + LAG + 1):
        if turn <= RIGHT:
            ring_step(0, turn)
        if turn == 0:
            normed_copies = spread_normed()
        if turn == RIGHT - 1:
            for copy in grads_copies + normed_copies:
                copy.wait_recv()
        if RIGHT - 1 <= turn < RIGHT - 1 + TILES and turn <= RIGHT + LAG:
            part_copies.append(part_tile(turn - RIGHT + 1))
        if turn >= LAG:
            ring_step(1, turn - LAG)
    for t in range(len(part_copies), TILES):
        part_copies.append(part_tile(t))
    for copy in part_copies:
        copy.wait_recv()

    sums = {}

    def sum_step(step):
        for way, (device, steps, sign) in enumerate(((right, RIGHT, 1), (left, LEFT, -1))):
            if step >= steps:
                continue
            for half in range(NY):
                pair_index = half * NZ + shift_z(sign * (steps - step))
                value = part[pair_index, core] + part_in[pair_index]
                if step > 0:
                    sums[way, half, step - 1].wait_recv()
                    value += land[way, step - 1, half]
                part[pair_index, core] = value
                sums[way, half, step] = start(
                    remote(
                        part.at[pair_index, core],
                        land.at[way, step, half],
                        sum_send.at[way, step, half],
                        sum_recv.at[way, step, half],
                        device,
                    )
                )

    sum_step(0)
    for copy in shares:
        copy.wait_recv()

    @pl.loop(0, NX)
    def _(j):
        total = None
        for half in range(2):
            term = lax.dot_general(
                grads[:, pl.ds(half * HALF, HALF)],
                weight[half, j].reshape(COLS, HALF),
                (((1,), (1,)), ((), ())),
                preferred_element_type=jnp.float32,
            )
            total = term if total is None else total + term
        normed_grad[j] = total

    load_residual.wait()
    passes = []
    for c in range(CHUNKS):
        passes.append(
            remote(
                result.at[pl.ds(c * CHUNK, CHUNK)],
                passed.at[0, pl.ds(c * CHUNK, CHUNK)],
                pass_send.at[c],
                pass_recv.at[c],
                before,
            )
        )

    def input_grad(c):
        rows = pl.ds(c * CHUNK, CHUNK)
        scale = scales[rows, 0:1]
        total = jnp.zeros((CHUNK, 1), jnp.float32)
        for j in range(NX):
            cols = pl.ds(j * COLS, COLS)
            h = hid[rows, cols].astype(jnp.float32)
            weighted = normed_grad[j, rows, :] * gains[:, cols]
            total += jnp.sum(weighted * h, axis=-1, keepdims=True)
        factor = total / D * scale * scale * scale
        for j in range(NX):
            cols = pl.ds(j * COLS, COLS)
            h = hid[rows, cols].astype(jnp.float32)
            weighted = normed_grad[j, rows, :] * gains[:, cols]
            value = weighted * scale - h * factor + res[rows, cols].astype(jnp.float32)
            result[rows, cols] = value.astype(jnp.bfloat16)
        passes[c].start()

    @pl.when(s > 0)
    def _():
        for c in range(CHUNKS):
            input_grad(c)

    blanks = [
        pltpu.make_async_copy(zeros, passed.at[0, pl.ds(c * CHUNK, CHUNK)], pass_recv.at[c])
        for c in range(CHUNKS)
    ]

    @pl.when(s == NS - 1)
    def _():
        zeros[...] = jnp.zeros_like(zeros)
        for copy in blanks:
            copy.start()

    for step in range(1, RIGHT):
        sum_step(step)

    totals = []
    for half in range(NY):
        pair_index = half * NZ + z
        sums[0, half, RIGHT - 1].wait_recv()
        sums[1, half, LEFT - 1].wait_recv()
        value = part[pair_index, core] + part_in[pair_index]
        value += land[0, RIGHT - 1, half] + land[1, LEFT - 1, half]
        part[pair_index, core] = value
    over = start(
        remote(part.at[(1 - y) * NZ + z, core], across, across_sem.at[0], across_sem.at[1], mirror)
    )
    over.wait_recv()
    grad_w[0] = (part[y * NZ + z, core] + across[...]) / math.sqrt(total_tokens)

    @pl.when(s < NS - 1)
    def _():
        for copy in passes:
            copy.wait_recv()

    @pl.when(s == NS - 1)
    def _():
        for copy in blanks:
            copy.wait()

    for copy in sent:
        copy.wait_send()

    @pl.when(s > 0)
    def _():
        for copy in passes:
            copy.wait_send()


def body(hidden, gain, key_grad, residual_grad, key_weight):
    total_tokens = hidden.shape[1] * lax.axis_size("fsdp")
    bf16, f32 = jnp.bfloat16, jnp.float32
    dma = pltpu.SemaphoreType.DMA
    return pl.pallas_call(
        functools.partial(kernel, total_tokens),
        out_shape=(
            jax.ShapeDtypeStruct((1, TOK, D), bf16),
            jax.ShapeDtypeStruct((1, ROWS, KW), f32),
        ),
        in_specs=[
            pl.BlockSpec(memory_space=pl.ANY),
            pl.BlockSpec(memory_space=pltpu.VMEM),
            pl.BlockSpec(memory_space=pl.ANY),
            pl.BlockSpec(memory_space=pl.ANY),
            pl.BlockSpec(memory_space=pltpu.VMEM),
        ],
        out_specs=(
            pl.BlockSpec(memory_space=pl.ANY),
            pl.BlockSpec(memory_space=pltpu.VMEM),
        ),
        scratch_shapes=[
            pltpu.VMEM((TOK, D), bf16),
            pltpu.VMEM((TOK, D), bf16),
            pltpu.VMEM((TOK, KW), bf16),
            pltpu.VMEM((1, D), f32),
            pltpu.VMEM((TOK, 128), f32),
            pltpu.VMEM((CHUNK, D), bf16),
            pltpu.VMEM((2, ROWS, KW), f32),
            pltpu.VMEM((2, NX, NY, NZ, 2 * ROWS, HALF), bf16),
            pltpu.VMEM((NX, TOK, COLS), bf16),
            pltpu.VMEM((NX, TOK, COLS), bf16),
            pltpu.VMEM((NX, TOK, KW), bf16),
            pltpu.VMEM((NY * NZ, 2, ROWS, KW), f32),
            pltpu.VMEM((NY * NZ, ROWS, KW), f32),
            pltpu.VMEM((2, RIGHT, NY, ROWS, KW), f32),
            pltpu.VMEM((ROWS, KW), f32),
            pltpu.VMEM((NX, TOK, COLS), f32),
            pltpu.VMEM((TOK, D), bf16),
            dma((3,)),
            dma((2,)),
            dma((2,)),
            dma((2, NX - 1)),
            dma((2, NX - 1)),
            dma((2, 2, RIGHT)),
            dma((2, 2, RIGHT)),
            dma((2, NZ)),
            dma((2, NZ)),
            dma((NX - 1,)),
            dma((NX - 1,)),
            dma((NX - 1,)),
            dma((NX - 1,)),
            dma((TILES,)),
            dma((TILES,)),
            dma((2, RIGHT, NY)),
            dma((2, RIGHT, NY)),
            dma((2,)),
            dma((CHUNKS,)),
            dma((CHUNKS,)),
        ],
        compiler_params=pltpu.CompilerParams(
            collective_id=0, has_side_effects=True, vmem_limit_bytes=60 * 2**20
        ),
        cost_estimate=pl.CostEstimate(
            flops=4 * TOK * D * KW, bytes_accessed=16 * 2**20, transcendentals=TOK
        ),
        name="key_backward",
    )(hidden, gain, key_grad, residual_grad, key_weight)


def solution(mesh):
    return jax.shard_map(
        body,
        mesh=mesh,
        in_specs=(
            P("section", "fsdp", None),
            P("section", None),
            P("section", "fsdp", None),
            P("section", "fsdp", None),
            P("section", "fsdp", None),
        ),
        out_specs=(P("section", "fsdp", None), P("section", "fsdp", None)),
        check_vma=False,
    )
```

time: 698 us -> 106 us (0.15)
  waiting for transfers between devices: 658 us -> 0 us
  Pallas kernels: 0 us -> 102 us
  between operations: 14.1 us -> 0.65 us
  matrix products: 10.9 us -> 0 us
    reduce_scatter x1 -> x0, waiting for transfers between devices: 427 us -> none  [body(): lax.psum_scatter(lax.dot_general(normed, grads, (((0,), (0,)), ((), ())),...]
    all_gather x1 -> x0, waiting for transfers between devices: 202 us -> none  [body(): lax.all_gather(key_weight[0], 'fsdp', axis=0, tiled=True)]
    pallas_call x0 -> x1, Pallas kernels: none -> 102 us  [body(): pl.pallas_call(functools.partial(kernel, total_tokens), out_shape=(jax.Sh...]
    ppermute x1 -> x0, waiting for transfers between devices: 27.9 us -> none  [passed_along(): return lax.ppermute(x, axis, pairs)]
    dot_general x2 -> x0, matrix products: 10.9 us -> none  [the longest x1 5.77 us: body(): lax.dot_general(grads, lax.all_gather(key_weight[0], 'fsdp', axis=0, tile...]
  transfers between devices with their start and end apart: 3 -> 0, of which waited for: 3 -> 0; matrix products, arithmetic and copies ran while one was open for 0% -> 0% of each run, Pallas kernels for 0% -> 0%
where the time goes in v1:
time: 106 us
  Pallas kernels  102 us (96%)
  local copies, waits for them, and re-layouts  3 us (3%)
    pallas_call x1, Pallas kernels, body(): pl.pallas_call(functools.partial(kernel, total_tokens), out_shape=(jax.Sh...  102 us
    unnamed x4, local copies, waits for them, and re-layouts  3 us

profile of v1, /device:TPU:1, one launch (start us, length us, event | category | flops | bytes accessed | tf_op | source)
XLA Modules:
  0.0 105.9 jit_solution(6491297386504097332)
XLA Ops:
  0.6 102.3 %key_backward.1 = (bf16[1,128,4608]{2,1,0:T(8,128)(2,1)}, f32[1,24,512]{2,1,0:T(8,128)}) custom-call(bf16[1,128,4608]{2,1,0:T(8,128)(2,1)} %hidden.1, bf16[1,4608]{1,0:T(2,128)(2,1)} %gain.1, bf16[1,128,512]{2,1,0:T(8,128)(2,1)} %key_grad.1, bf16[1,128,4608]{2,1,0:T(8,128)(2,1)} %residual.1, bf16[1,24,512]{2,1,0:T(8,128)(2,1)} %key_weight.1), custom_call_target="tpu_custom_call" | custom-call | flops 1207959552 | bytes 16777216 | tf_op jit(solution)/shard_map/key_backward/pallas_call | solution.py:382
  102.9 0.0 copy-start
  102.9 2.4 %copy.9 = bf16[1,128,4608]{2,1,0:T(8,128)(2,1)} copy(bf16[1,128,4608]{2,1,0:T(8,128)(2,1)} %get-tuple-element.4) | data formatting | bytes 2359296
  105.3 0.0 copy-done
  105.3 0.6 copy.10
Async XLA Ops:
  102.9 2.4 %copy-start = (f32[1,24,512]{2,1,0:T(8,128)S(1)}, f32[1,24,512]{2,1,0:T(8,128)}, u32[]{:S(2)}) copy-start(f32[1,24,512]{2,1,0:T(8,128)} %get-tuple-element.5) | copy-start | bytes 147460

commit v2 on v1

--- a/solution.py
+++ b/solution.py
@@ -12,7 +12,8 @@
 NX, NY, NZ, NS = 4, 2, 12, 4
 RIGHT, LEFT = NZ // 2, (NZ - 1) // 2
 TOK, KW, ROWS = 128, 512, 24
-HALF = KW // 2
+QUARTER = KW // 4
+PIECES, PIECE = 2, KW // 2
 COLS = NY * NZ * 2 * ROWS
 D = NX * COLS
 TILE = 384
@@ -21,6 +22,7 @@
 CHUNK = 16
 CHUNKS = TOK // CHUNK
 LAG = 1
+SEND_NORMED = 2
 
 
 def kernel(
@@ -34,6 +36,8 @@
     grad_w,
     hid,
     res,
+    gain_in,
+    weight_in,
     grads,
     gains,
     scales,
@@ -58,6 +62,8 @@
     z_recv,
     share_send,
     share_recv,
+    late_send,
+    late_recv,
     grads_send,
     grads_recv,
     normed_send,
@@ -66,7 +72,8 @@
     part_recv,
     sum_send,
     sum_recv,
-    across_sem,
+    across_send,
+    across_recv,
     pass_send,
     pass_recv,
 ):
@@ -107,6 +114,10 @@
     load_hidden.start()
     load_grads.start()
     load_residual.start()
+    load_gain = pltpu.make_async_copy(gain, gain_in, load_sem.at[3])
+    load_weight = pltpu.make_async_copy(key_weight, weight_in, load_sem.at[4])
+    load_gain.start()
+    load_weight.start()
 
     barrier = pltpu.get_barrier_semaphore()
     for device in [sibling, mirror, right, left] + others:
@@ -116,8 +127,10 @@
     def _():
         pl.semaphore_signal(barrier, 1, device_id=after, device_id_type=MESH)
 
-    pair[core] = key_weight[0].astype(jnp.float32)
-    gains[...] = gain[...].astype(jnp.float32)
+    load_weight.wait()
+    pair[core] = weight_in[0].astype(jnp.float32)
+    load_gain.wait()
+    gains[...] = gain_in[...].astype(jnp.float32)
     pl.semaphore_wait(barrier, 4 + len(others) + jnp.minimum(s, 1))
 
     sent = []
@@ -130,33 +143,94 @@
     swap = start(remote(pair.at[core], pair.at[core], pair_sem.at[0], pair_sem.at[1], sibling))
     swap.wait_recv()
     block = pair[...].reshape(2 * ROWS, KW)
-    weight[core, x, y, z] = jnp.where(core == 0, block[:, :HALF], block[:, HALF:]).astype(jnp.bfloat16)
-
-    def own(plane):
-        return weight.at[core, x, plane, z]
-
-    def spread_x(plane, index):
+    for h in range(2):
+        quarters = [block[:, q * QUARTER : (q + 1) * QUARTER] for q in (h, 2 + h)]
+        weight[2 * core + h, x, y, z] = jnp.where(core == 0, *quarters).astype(jnp.bfloat16)
+
+    planes = [y, 1 - y]
+    first, second = 2 * core, 2 * core + 1
+    both = weight.at[pl.ds(first, 2), x, y, z]
+    to_mirror = start(remote(both, both, y_sem.at[0], y_sem.at[1], mirror))
+
+    def spread_x(index):
+        own = weight.at[first, x, planes[index], z]
         return [
-            start(remote(own(plane), own(plane), x_send.at[index, k], x_recv.at[index, k], others[k]))
+            start(remote(own, own, x_send.at[index, k], x_recv.at[index, k], others[k]))
             for k in range(NX - 1)
         ]
 
-    planes = [y, 1 - y]
-    to_mirror = start(remote(own(y), own(y), y_sem.at[0], y_sem.at[1], mirror))
-    x_copies = [spread_x(y, 0), None]
+    x_copies = [spread_x(0), None]
+
+    ring = {}
+
+    def slot(h, index, by):
+        if h == 0:
+            return weight.at[first, :, planes[index], shift_z(by)]
+        return weight.at[second, x, planes[index], shift_z(by)]
+
+    WAYS = ((right, RIGHT, -1), (left, LEFT, 1))
+
+    def ring_step(h, index, step):
+        if step == 0:
+            if index == 1 and h == 1:
+                to_mirror.wait_recv()
+                x_copies[1] = spread_x(1)
+            if h == 0:
+                for copy in x_copies[index]:
+                    copy.wait_recv()
+        for way, (device, steps, sign) in enumerate(WAYS):
+            if 0 < step <= steps:
+                ring[h, way, index, step - 1].wait_recv()
+            if step < steps:
+                ring[h, way, index, step] = start(
+                    remote(
+                        slot(h, index, sign * step),
+                        slot(h, index, sign * step),
+                        z_send.at[h, way, index, step],
+                        z_recv.at[h, way, index, step],
+                        device,
+                    )
+                )
+
+    def arrived(step):
+        return [
+            (sign * step, step if way == 0 else RIGHT + step)
+            for way, (_, steps, sign) in enumerate(WAYS)
+            if step <= steps and (step > 0 or way == 0)
+        ]
+
+    shares, spread = [], {}
+
+    def share(h, step):
+        for by, order in arrived(step):
+            if h == 1:
+                for copy in spread[order]:
+                    copy.wait_recv()
+            both_planes = weight.at[2 * core + h, :, :, shift_z(by)]
+            shares.append(
+                start(
+                    remote(both_planes, both_planes, share_send.at[h, order], share_recv.at[h, order], sibling)
+                )
+            )
+
+    def spread_late(step):
+        for by, order in arrived(step):
+            mine = weight.at[second, x, :, shift_z(by)]
+            spread[order] = [
+                start(remote(mine, mine, late_send.at[order, k], late_recv.at[order, k], others[k]))
+                for k in range(NX - 1)
+            ]
+
+    ring_step(1, 0, 0)
 
     load_grads.wait()
     grads_copies = [
         start(remote(grads, grads_in.at[x], grads_send.at[k], grads_recv.at[k], others[k]))
         for k in range(NX - 1)
     ]
-    grads_in[x] = grads[...]
-
-    load_hidden.wait()
-
-    @pl.loop(0, CHUNKS)
-    def _(c):
-        rows = pl.ds(pl.multiple_of(c * CHUNK, CHUNK), CHUNK)
+
+    def normalise(c):
+        rows = pl.ds(c * CHUNK, CHUNK)
         total = jnp.zeros((CHUNK, 1), jnp.float32)
         for j in range(NX):
             h = hid[rows, pl.ds(j * COLS, COLS)].astype(jnp.float32)
@@ -177,43 +251,30 @@
                     remote(normed_out.at[to], normed_in.at[x], normed_send.at[k], normed_recv.at[k], others[k])
                 )
             )
-        normed_in[x] = normed_out[x]
         return copies
 
-    def slot(index, by):
-        return weight.at[core, :, planes[index], shift_z(by)]
-
-    def share(index, by, order):
-        return start(
-            remote(slot(index, by), slot(index, by), share_send.at[index, order], share_recv.at[index, order], sibling)
-        )
-
-    shares, ring = [], {}
-
-    def ring_step(index, step):
-        if step == 0:
-            if index == 1:
-                to_mirror.wait_recv()
-                x_copies[1] = spread_x(planes[1], 1)
-            for copy in x_copies[index]:
-                copy.wait_recv()
-        for way, (device, steps, sign) in enumerate(((right, RIGHT, -1), (left, LEFT, 1))):
-            if 0 < step <= steps:
-                ring[way, index, step - 1].wait_recv()
-            if step < steps:
-                ring[way, index, step] = start(
-                    remote(
-                        slot(index, sign * step),
-                        slot(index, sign * step),
-                        z_send.at[way, index, step],
-                        z_recv.at[way, index, step],
-                        device,
-                    )
-                )
-            if step == 0 and way == 0:
-                shares.append(share(index, 0, 0))
-            if 0 < step <= steps:
-                shares.append(share(index, sign * step, step if way == 0 else RIGHT + step))
+    load_hidden.wait()
+    per_turn = CHUNKS // SEND_NORMED
+    for turn in range(RIGHT + LAG + 3):
+        if turn <= RIGHT:
+            ring_step(0, 0, turn)
+            if turn < RIGHT:
+                ring_step(1, 0, turn + 1)
+        if 0 <= turn - LAG <= RIGHT:
+            ring_step(1, 1, turn - LAG)
+            spread_late(turn - LAG)
+            ring_step(0, 1, turn - LAG)
+            share(0, turn - LAG)
+        if 0 <= turn - LAG - 1 <= RIGHT:
+            share(1, turn - LAG - 1)
+        if turn < SEND_NORMED:
+            for c in range(turn * per_turn, (turn + 1) * per_turn):
+                normalise(c)
+        if turn == SEND_NORMED:
+            normed_copies = spread_normed()
+
+    grads_in[x] = grads[...]
+    normed_in[x] = normed_out[x]
 
     def part_tile(t):
         lhs = normed_in[:, :, pl.ds(t * TILE, TILE)].reshape(NX * TOK, TILE)
@@ -234,63 +295,45 @@
             )
         )
 
-    part_copies = []
-    for turn in range(RIGHT + LAG + 1):
-        if turn <= RIGHT:
-            ring_step(0, turn)
-        if turn == 0:
-            normed_copies = spread_normed()
-        if turn == RIGHT - 1:
-            for copy in grads_copies + normed_copies:
-                copy.wait_recv()
-        if RIGHT - 1 <= turn < RIGHT - 1 + TILES and turn <= RIGHT + LAG:
-            part_copies.append(part_tile(turn - RIGHT + 1))
-        if turn >= LAG:
-            ring_step(1, turn - LAG)
-    for t in range(len(part_copies), TILES):
-        part_copies.append(part_tile(t))
-    for copy in part_copies:
-        copy.wait_recv()
-
+    halves = [1 - y, y]
     sums = {}
 
+    def own_sum(half, by, piece):
+        pair_index = halves[half] * NZ + shift_z(by)
+        cols = pl.ds(piece * PIECE, PIECE)
+        return part.at[pair_index, core, :, cols], part_in[pair_index, :, cols]
+
     def sum_step(step):
-        for way, (device, steps, sign) in enumerate(((right, RIGHT, 1), (left, LEFT, -1))):
-            if step >= steps:
-                continue
-            for half in range(NY):
-                pair_index = half * NZ + shift_z(sign * (steps - step))
-                value = part[pair_index, core] + part_in[pair_index]
-                if step > 0:
-                    sums[way, half, step - 1].wait_recv()
-                    value += land[way, step - 1, half]
-                part[pair_index, core] = value
-                sums[way, half, step] = start(
-                    remote(
-                        part.at[pair_index, core],
-                        land.at[way, step, half],
-                        sum_send.at[way, step, half],
-                        sum_recv.at[way, step, half],
-                        device,
+        for half in range(NY):
+            for piece in range(PIECES):
+                for way, (device, steps, sign) in enumerate(WAYS):
+                    if step >= steps:
+                        continue
+                    mine, other = own_sum(half, sign * (step - steps), piece)
+                    value = mine[...] + other
+                    if step > 0:
+                        sums[way, half, piece, step - 1].wait_recv()
+                        value += land[way, step - 1, half, piece]
+                    mine[...] = value
+                    sums[way, half, piece, step] = start(
+                        remote(
+                            mine,
+                            land.at[way, step, half, piece],
+                            sum_send.at[way, step, half, piece],
+                            sum_recv.at[way, step, half, piece],
+                            device,
+                        )
                     )
-                )
-
-    sum_step(0)
+
     for copy in shares:
         copy.wait_recv()
 
     @pl.loop(0, NX)
     def _(j):
-        total = None
-        for half in range(2):
-            term = lax.dot_general(
-                grads[:, pl.ds(half * HALF, HALF)],
-                weight[half, j].reshape(COLS, HALF),
-                (((1,), (1,)), ((), ())),
-                preferred_element_type=jnp.float32,
-            )
-            total = term if total is None else total + term
-        normed_grad[j] = total
+        rows = jnp.concatenate([weight[q, j].reshape(COLS, QUARTER) for q in range(4)], axis=1)
+        normed_grad[j] = lax.dot_general(
+            grads[...], rows, (((1,), (1,)), ((), ())), preferred_element_type=jnp.float32
+        )
 
     load_residual.wait()
     passes = []
@@ -339,22 +382,30 @@
         for copy in blanks:
             copy.start()
 
-    for step in range(1, RIGHT):
+    for copy in grads_copies + normed_copies:
+        copy.wait_recv()
+    part_copies = [part_tile(t) for t in range(TILES)]
+    for copy in part_copies:
+        copy.wait_recv()
+    for step in range(RIGHT):
         sum_step(step)
 
-    totals = []
+    finals = []
     for half in range(NY):
-        pair_index = half * NZ + z
-        sums[0, half, RIGHT - 1].wait_recv()
-        sums[1, half, LEFT - 1].wait_recv()
-        value = part[pair_index, core] + part_in[pair_index]
-        value += land[0, RIGHT - 1, half] + land[1, LEFT - 1, half]
-        part[pair_index, core] = value
-    over = start(
-        remote(part.at[(1 - y) * NZ + z, core], across, across_sem.at[0], across_sem.at[1], mirror)
-    )
-    over.wait_recv()
-    grad_w[0] = (part[y * NZ + z, core] + across[...]) / math.sqrt(total_tokens)
+        for piece in range(PIECES):
+            mine, other = own_sum(half, 0, piece)
+            value = mine[...] + other
+            for way, (_, steps, _) in enumerate(WAYS):
+                sums[way, half, piece, steps - 1].wait_recv()
+                value += land[way, steps - 1, half, piece]
+            if half == 0:
+                mine[...] = value
+                finals.append(
+                    start(remote(mine, across.at[piece], across_send.at[piece], across_recv.at[piece], mirror))
+                )
+            else:
+                finals[piece].wait_recv()
+                grad_w[0, :, pl.ds(piece * PIECE, PIECE)] = (value + across[piece]) / math.sqrt(total_tokens)
 
     @pl.when(s < NS - 1)
     def _():
@@ -387,10 +438,10 @@
         ),
         in_specs=[
             pl.BlockSpec(memory_space=pl.ANY),
-            pl.BlockSpec(memory_space=pltpu.VMEM),
             pl.BlockSpec(memory_space=pl.ANY),
             pl.BlockSpec(memory_space=pl.ANY),
-            pl.BlockSpec(memory_space=pltpu.VMEM),
+            pl.BlockSpec(memory_space=pl.ANY),
+            pl.BlockSpec(memory_space=pl.ANY),
         ],
         out_specs=(
             pl.BlockSpec(memory_space=pl.ANY),
@@ -399,39 +450,44 @@
         scratch_shapes=[
             pltpu.VMEM((TOK, D), bf16),
             pltpu.VMEM((TOK, D), bf16),
+            pltpu.VMEM((1, D), bf16),
+            pltpu.VMEM((1, ROWS, KW), bf16),
             pltpu.VMEM((TOK, KW), bf16),
             pltpu.VMEM((1, D), f32),
             pltpu.VMEM((TOK, 128), f32),
             pltpu.VMEM((CHUNK, D), bf16),
             pltpu.VMEM((2, ROWS, KW), f32),
-            pltpu.VMEM((2, NX, NY, NZ, 2 * ROWS, HALF), bf16),
+            pltpu.VMEM((4, NX, NY, NZ, 2 * ROWS, QUARTER), bf16),
             pltpu.VMEM((NX, TOK, COLS), bf16),
             pltpu.VMEM((NX, TOK, COLS), bf16),
             pltpu.VMEM((NX, TOK, KW), bf16),
             pltpu.VMEM((NY * NZ, 2, ROWS, KW), f32),
             pltpu.VMEM((NY * NZ, ROWS, KW), f32),
-            pltpu.VMEM((2, RIGHT, NY, ROWS, KW), f32),
-            pltpu.VMEM((ROWS, KW), f32),
+            pltpu.VMEM((2, RIGHT, NY, PIECES, ROWS, PIECE), f32),
+            pltpu.VMEM((PIECES, ROWS, PIECE), f32),
             pltpu.VMEM((NX, TOK, COLS), f32),
             pltpu.VMEM((TOK, D), bf16),
-            dma((3,)),
+            dma((5,)),
             dma((2,)),
             dma((2,)),
             dma((2, NX - 1)),
             dma((2, NX - 1)),
-            dma((2, 2, RIGHT)),
-            dma((2, 2, RIGHT)),
+            dma((2, 2, 2, RIGHT)),
+            dma((2, 2, 2, RIGHT)),
             dma((2, NZ)),
             dma((2, NZ)),
+            dma((NZ, NX - 1)),
+            dma((NZ, NX - 1)),
             dma((NX - 1,)),
             dma((NX - 1,)),
             dma((NX - 1,)),
             dma((NX - 1,)),
             dma((TILES,)),
             dma((TILES,)),
-            dma((2, RIGHT, NY)),
-            dma((2, RIGHT, NY)),
-            dma((2,)),
+            dma((2, RIGHT, NY, PIECES)),
+            dma((2, RIGHT, NY, PIECES)),
+            dma((PIECES,)),
+            dma((PIECES,)),
             dma((CHUNKS,)),
             dma((CHUNKS,)),
         ],

time: 106 us -> 102 us (0.962)
  the two profiles are of different devices: /device:TPU:1 before, /device:TPU:9 now
where the time goes in v2:
time: 102 us
  Pallas kernels  98.6 us (97%)
  local copies, waits for them, and re-layouts  3 us (3%)
    pallas_call x1, Pallas kernels, body(): pl.pallas_call(functools.partial(kernel, total_tokens), out_shape=(jax.Sh...  98.6 us
    unnamed x4, local copies, waits for them, and re-layouts  3 us

profile of v2, /device:TPU:9, one launch (start us, length us, event | category | flops | bytes accessed | tf_op | source)
XLA Modules:
  0.0 102.2 jit_solution(16041287515434236540)
XLA Ops:
  0.6 98.6 %key_backward.1 = (bf16[1,128,4608]{2,1,0:T(8,128)(2,1)}, f32[1,24,512]{2,1,0:T(8,128)}) custom-call(bf16[1,128,4608]{2,1,0:T(8,128)(2,1)} %hidden.1, bf16[1,4608]{1,0:T(2,128)(2,1)} %gain.1, bf16[1,128,512]{2,1,0:T(8,128)(2,1)} %key_grad.1, bf16[1,128,4608]{2,1,0:T(8,128)(2,1)} %residual.1, bf16[1,24,512]{2,1,0:T(8,128)(2,1)} %key_weight.1), custom_call_target="tpu_custom_call" | custom-call | flops 1207959552 | bytes 16777216 | tf_op jit(solution)/shard_map/key_backward/pallas_call | solution.py:433
  99.2 0.0 copy-start
  99.2 2.4 %copy.9 = bf16[1,128,4608]{2,1,0:T(8,128)(2,1)} copy(bf16[1,128,4608]{2,1,0:T(8,128)(2,1)} %get-tuple-element.4) | data formatting | bytes 2359296
  101.6 0.0 copy-done
  101.6 0.6 copy.10
Async XLA Ops:
  99.2 2.4 %copy-start = (f32[1,24,512]{2,1,0:T(8,128)S(1)}, f32[1,24,512]{2,1,0:T(8,128)}, u32[]{:S(2)}) copy-start(f32[1,24,512]{2,1,0:T(8,128)} %get-tuple-element.5) | copy-start | bytes 147460

commit v3 on v2

--- a/solution.py
+++ b/solution.py
@@ -21,8 +21,8 @@
 PAIRS = TILE // (2 * ROWS)
 CHUNK = 16
 CHUNKS = TOK // CHUNK
-LAG = 1
-SEND_NORMED = 2
+LAG, LATE_LAG = 2, 1
+PER_TURN = 1
 
 
 def kernel(
@@ -242,39 +242,25 @@
             normed = h * scale * gains[:, pl.ds(j * COLS, COLS)]
             normed_out[j, rows, :] = normed.astype(jnp.bfloat16)
 
-    def spread_normed():
-        copies = []
-        for k in range(NX - 1):
+    normed_copies = []
+
+    def spread_normed(c):
+        rows = pl.ds(c * CHUNK, CHUNK)
+        for k in (0, 2, 1):
             to = lax.rem(x + k + 1, NX)
-            copies.append(
+            normed_copies.append(
                 start(
-                    remote(normed_out.at[to], normed_in.at[x], normed_send.at[k], normed_recv.at[k], others[k])
+                    remote(
+                        normed_out.at[to, rows],
+                        normed_in.at[x, rows],
+                        normed_send.at[c, k],
+                        normed_recv.at[c, k],
+                        others[k],
+                    )
                 )
             )
-        return copies
 
     load_hidden.wait()
-    per_turn = CHUNKS // SEND_NORMED
-    for turn in range(RIGHT + LAG + 3):
-        if turn <= RIGHT:
-            ring_step(0, 0, turn)
-            if turn < RIGHT:
-                ring_step(1, 0, turn + 1)
-        if 0 <= turn - LAG <= RIGHT:
-            ring_step(1, 1, turn - LAG)
-            spread_late(turn - LAG)
-            ring_step(0, 1, turn - LAG)
-            share(0, turn - LAG)
-        if 0 <= turn - LAG - 1 <= RIGHT:
-            share(1, turn - LAG - 1)
-        if turn < SEND_NORMED:
-            for c in range(turn * per_turn, (turn + 1) * per_turn):
-                normalise(c)
-        if turn == SEND_NORMED:
-            normed_copies = spread_normed()
-
-    grads_in[x] = grads[...]
-    normed_in[x] = normed_out[x]
 
     def part_tile(t):
         lhs = normed_in[:, :, pl.ds(t * TILE, TILE)].reshape(NX * TOK, TILE)
@@ -294,6 +280,25 @@
                 sibling,
             )
         )
+
+    for turn in range(RIGHT + LAG + 1):
+        if turn <= RIGHT:
+            ring_step(0, 0, turn)
+            if turn < RIGHT:
+                ring_step(1, 0, turn + 1)
+        if 0 <= turn - LATE_LAG <= RIGHT:
+            ring_step(1, 1, turn - LATE_LAG)
+        if 0 <= turn - LAG <= RIGHT:
+            ring_step(0, 1, turn - LAG)
+        if 0 <= turn - LATE_LAG <= RIGHT:
+            spread_late(turn - LATE_LAG)
+        if 0 <= turn - LAG <= RIGHT:
+            share(0, turn - LAG)
+        if 0 <= turn - LATE_LAG - 1 <= RIGHT:
+            share(1, turn - LATE_LAG - 1)
+        for c in range(turn * PER_TURN, min((turn + 1) * PER_TURN, CHUNKS)):
+            normalise(c)
+            spread_normed(c)
 
     halves = [1 - y, y]
     sums = {}
@@ -382,6 +387,8 @@
         for copy in blanks:
             copy.start()
 
+    grads_in[x] = grads[...]
+    normed_in[x] = normed_out[x]
     for copy in grads_copies + normed_copies:
         copy.wait_recv()
     part_copies = [part_tile(t) for t in range(TILES)]
@@ -480,8 +487,8 @@
             dma((NZ, NX - 1)),
             dma((NX - 1,)),
             dma((NX - 1,)),
-            dma((NX - 1,)),
-            dma((NX - 1,)),
+            dma((CHUNKS, NX - 1)),
+            dma((CHUNKS, NX - 1)),
             dma((TILES,)),
             dma((TILES,)),
             dma((2, RIGHT, NY, PIECES)),

time: 102 us -> 94.9 us (0.930)
  the two profiles are of different devices: /device:TPU:9 before, /device:TPU:1 now
where the time goes in v3:
time: 94.9 us; the launch traced here: 93.9 us
  Pallas kernels  90.2 us (95%)
  local copies, waits for them, and re-layouts  3 us (3%)
    pallas_call x1, Pallas kernels, body(): pl.pallas_call(functools.partial(kernel, total_tokens), out_shape=(jax.Sh...  90.2 us
    unnamed x4, local copies, waits for them, and re-layouts  3 us

profile of v3, /device:TPU:1, one launch (start us, length us, event | category | flops | bytes accessed | tf_op | source)
XLA Modules:
  0.0 93.9 jit_solution(5718068691036585793)
XLA Ops:
  0.6 90.2 %key_backward.1 = (bf16[1,128,4608]{2,1,0:T(8,128)(2,1)}, f32[1,24,512]{2,1,0:T(8,128)}) custom-call(bf16[1,128,4608]{2,1,0:T(8,128)(2,1)} %hidden.1, bf16[1,4608]{1,0:T(2,128)(2,1)} %gain.1, bf16[1,128,512]{2,1,0:T(8,128)(2,1)} %key_grad.1, bf16[1,128,4608]{2,1,0:T(8,128)(2,1)} %residual.1, bf16[1,24,512]{2,1,0:T(8,128)(2,1)} %key_weight.1), custom_call_target="tpu_custom_call" | custom-call | flops 1207959552 | bytes 16777216 | tf_op jit(solution)/shard_map/key_backward/pallas_call | solution.py:440
  90.9 0.0 copy-start
  90.9 2.4 %copy.9 = bf16[1,128,4608]{2,1,0:T(8,128)(2,1)} copy(bf16[1,128,4608]{2,1,0:T(8,128)(2,1)} %get-tuple-element.4) | data formatting | bytes 2359296
  93.2 0.0 copy-done
  93.3 0.6 copy.10
Async XLA Ops:
  90.9 2.4 %copy-start = (f32[1,24,512]{2,1,0:T(8,128)S(1)}, f32[1,24,512]{2,1,0:T(8,128)}, u32[]{:S(2)}) copy-start(f32[1,24,512]{2,1,0:T(8,128)} %get-tuple-element.5) | copy-start | bytes 147460

commit v4 on v3

--- a/solution.py
+++ b/solution.py
@@ -224,10 +224,7 @@
     ring_step(1, 0, 0)
 
     load_grads.wait()
-    grads_copies = [
-        start(remote(grads, grads_in.at[x], grads_send.at[k], grads_recv.at[k], others[k]))
-        for k in range(NX - 1)
-    ]
+    grads_copies = []
 
     def normalise(c):
         rows = pl.ds(c * CHUNK, CHUNK)
@@ -296,6 +293,11 @@
             share(0, turn - LAG)
         if 0 <= turn - LATE_LAG - 1 <= RIGHT:
             share(1, turn - LATE_LAG - 1)
+        if 0 < turn < NX:
+            k = turn - 1
+            grads_copies.append(
+                start(remote(grads, grads_in.at[x], grads_send.at[k], grads_recv.at[k], others[k]))
+            )
         for c in range(turn * PER_TURN, min((turn + 1) * PER_TURN, CHUNKS)):
             normalise(c)
             spread_normed(c)

time: 94.9 us -> 98.4 us (1.037)
  Pallas kernels: 90.2 us -> 94.6 us
    pallas_call x1, Pallas kernels: 90.2 us -> 94.6 us  [body(): pl.pallas_call(functools.partial(kernel, total_tokens), out_shape=(jax.Sh...]
where the time goes in v4:
time: 98.4 us; the launch traced here: 98.2 us
  Pallas kernels  94.6 us (96%)
  local copies, waits for them, and re-layouts  3 us (3%)
    pallas_call x1, Pallas kernels, body(): pl.pallas_call(functools.partial(kernel, total_tokens), out_shape=(jax.Sh...  94.6 us
    unnamed x4, local copies, waits for them, and re-layouts  3 us

profile of v4, /device:TPU:1, one launch (start us, length us, event | category | flops | bytes accessed | tf_op | source)
XLA Modules:
  0.0 98.2 jit_solution(6224996167163977112)
XLA Ops:
  0.6 94.6 %key_backward.1 = (bf16[1,128,4608]{2,1,0:T(8,128)(2,1)}, f32[1,24,512]{2,1,0:T(8,128)}) custom-call(bf16[1,128,4608]{2,1,0:T(8,128)(2,1)} %hidden.1, bf16[1,4608]{1,0:T(2,128)(2,1)} %gain.1, bf16[1,128,512]{2,1,0:T(8,128)(2,1)} %key_grad.1, bf16[1,128,4608]{2,1,0:T(8,128)(2,1)} %residual.1, bf16[1,24,512]{2,1,0:T(8,128)(2,1)} %key_weight.1), custom_call_target="tpu_custom_call" | custom-call | flops 1207959552 | bytes 16777216 | tf_op jit(solution)/shard_map/key_backward/pallas_call | solution.py:442
  95.2 0.0 copy-start
  95.2 2.4 %copy.9 = bf16[1,128,4608]{2,1,0:T(8,128)(2,1)} copy(bf16[1,128,4608]{2,1,0:T(8,128)(2,1)} %get-tuple-element.4) | data formatting | bytes 2359296
  97.6 0.0 copy-done
  97.6 0.6 copy.10
Async XLA Ops:
  95.2 2.4 %copy-start = (f32[1,24,512]{2,1,0:T(8,128)S(1)}, f32[1,24,512]{2,1,0:T(8,128)}, u32[]{:S(2)}) copy-start(f32[1,24,512]{2,1,0:T(8,128)} %get-tuple-element.5) | copy-start | bytes 147460
